TPU v7x, 1024 devices: a whole 8x8x8 slice. The times are simulated.
1024 devices in a mesh: row: 64 (over z, x), col: 16 (over y, core).
Axes of the slice: x: 8, y: 8, z: 8, core: 2. Of those that a mesh axis runs over, the one named last changes fastest.
Arguments:
- features: bfloat16 [65536, 256], P(('row', 'col')), may hold values from -6 to 6
- tiles: bfloat16 [64, 16, 96, 128, 128], P('row', 'col'), may hold values from -0.0546875 to 0.0546875
- places: int32 [64, 16, 96], P('row', 'col'), may hold values from 0 to 255, as said below
- counts: int32 [64, 16], P('row', 'col'), may hold values from 24 to 96, as said below
- weight: bfloat16 [256, 256], replicated, may hold values from -0.375 to 0.375
Outputs:
- hidden_out: bfloat16 [65536, 256], P(('row', 'col'))
Inputs may be any that keep to these rules, and one draw needn't show every extreme that they name: `places`: slots below counts of a device hold its occupied tile positions, distinct and increasing; the other slots hold distinct unoccupied positions. `counts`: some device holds exactly 96 occupied tiles and some exactly 24.
All inputs are finite; a program needn't handle non-finite values.
Results may differ from a plain program's by a relative error of at most 0.0049.
Values may be sent and summed in bfloat16 or wider, within the bound.
A program may use at most 64 MiB of HBM per device.

v0:
```python
import jax
import jax.numpy as jnp
from jax import lax
from jax.sharding import PartitionSpec as P


def accumulate(partial_value, tile_list, place_list, x_tiles, slot_limit, block_size):
    tile_cols = x_tiles.shape[0]

    def add_block(block_index, running):
        first = block_index * block_size
        tile_block = lax.dynamic_slice_in_dim(tile_list, first, block_size, 0)
        place_block = lax.dynamic_slice_in_dim(place_list, first, block_size, 0)
        col_ids = place_block % tile_cols
        row_ids = place_block // tile_cols
        sources = jnp.take(x_tiles, col_ids, axis=0)
        products = jnp.einsum(
            "kab,kbf->kaf", tile_block, sources, preferred_element_type=jnp.float32
        )
        usable = first + jnp.arange(block_size, dtype=jnp.int32) < slot_limit
        masked = jnp.where(usable[:, None, None], products, jnp.float32(0.0))
        return running.at[row_ids].add(masked)

    block_count = (slot_limit + block_size - 1) // block_size
    return lax.fori_loop(0, block_count, add_block, partial_value)


def per_device(features, tiles, places, counts, weight):
    gathered = lax.all_gather(features, "col", axis=0, tiled=True)
    tile_list = tiles[0, 0]
    place_list = places[0, 0]
    own_count = counts[0, 0]
    tile_size = tile_list.shape[-1]
    feature_width = features.shape[1]
    master_rows = features.shape[0]
    block_size = min(32, tile_list.shape[0])
    tile_rows = lax.axis_size("row") * master_rows // tile_size
    x_tiles = gathered.reshape(gathered.shape[0] // tile_size, tile_size, feature_width)
    partial_value = jnp.zeros((tile_rows, tile_size, feature_width), jnp.float32)
    partial_value = accumulate(partial_value, tile_list, place_list, x_tiles, own_count, block_size)
    flat_rows = partial_value.reshape(tile_rows * tile_size, feature_width)
    summed = lax.psum_scatter(flat_rows, "row", scatter_dimension=0, tiled=True)
    aggregated = summed.astype(jnp.bfloat16)
    return jax.nn.relu(jnp.dot(aggregated, weight, preferred_element_type=jnp.float32)).astype(
        jnp.bfloat16
    )


def solution(mesh):
    return jax.shard_map(
        per_device,
        mesh=mesh,
        in_specs=(
            P(("row", "col"), None),
            P("row", "col", None, None, None),
            P("row", "col", None),
            P("row", "col"),
            P(),
        ),
        out_specs=P(("row", "col"), None),
        check_vma=False,
    )
```

profile of v0, /device:TPU:16, one launch (start us, length us, event | category | flops | bytes accessed | tf_op | source)
XLA Modules:
  0.0 343.9 jit_solution(15751769791644534995)
XLA Ops:
  6.5 0.0 copy-start
  6.5 0.0 copy-start.1
  6.5 0.0 reduce-scatter.2.cloned.1.call-start
  7.3 28.8 %all_gather.3 = bf16[1024,256]{1,0:T(8,128)(2,1)S(1)} all-gather(bf16[64,256]{1,0:T(8,128)(2,1)} %param.7), channel_id=1, replica_groups=mesh['row'=64,'col'=16] {'col'}, dimensions={0}, use_global_device_ids=true | all-gather | bytes 557056 | tf_op jit(solution)/shard_map/all_gather | solution.py:29
  36.0 2.4 broadcast_in_dim.50
  38.5 0.0 copy-done.1
  38.5 29.9 %while.12 = (s32[]{:T(128)}, f32[32,128,256]{2,1,0:T(8,128)}, s32[]{:T(128)}, s32[96]{0:T(128)S(1)}, s32[]{:T(128)}, /*index=5*/bf16[96,128,128]{2,1,0:T(8,128)(...) while((s32[]{:T(128)}, f32[32,128,256]{2,1,0:T(8,128)}, ...), condition=%wide.region_2.3_spmd, body=%wide.region_0.2_spmd.sunk | while | flops 271583296 | bytes 24122800 | solution.py:25
  38.5 0.7 compare_and_fusion.2
  39.2 0.1 compare_select_fusion.8
  39.3 0.7 gather_fusion
  40.0 3.9 %convolution_select_fusion.2 = f32[32,128,256]{2,1,0:T(8,128)} fusion(bf16[32,128,256]{2,1,0:T(8,128)(2,1)S(1)} %gather_fusion, pred[32]{0:T(512)(128)(4,1)S(1)} %get-tuple-element.169, pred[32]{0:T(512)(128)(4,1)S(1)} %get-tuple-element.170, bf16[96,128,128]{2,1,0:T(8,128)(2,1)} %get-tuple-element.198, s32[]{:T(128)S(6)} %select_n.82), kind=kOutput, calls=%fused_computation.2.clone.1 | convolution fusion | flops 270532608 | bytes 7340100 | tf_op jit(solution)/shard_map/while/body/kab,kbf->kaf/dot_general | solution.py:17
  43.9 9.5 %scatter_fusion = f32[32,128,256]{2,1,0:T(8,128)} fusion(f32[32,128,256]{2,1,0:T(8,128)} %get-tuple-element.183, s32[32]{0:T(128)S(1)} %compare_select_fusion.8, f32[32,128,256]{2,1,0:T(8,128)} %convolution_select_fusion.2), kind=kCustom, calls=%fused_computation.1.clone.1 | custom fusion | flops 1048576 | bytes 12583040 | tf_op jit(solution)/shard_map/while/body/scatter-add | solution.py:22
  53.5 0.7 compare_and_fusion.2
  54.2 0.1 compare_select_fusion.8
  54.3 0.7 gather_fusion
  55.0 3.9 %convolution_select_fusion.2 = f32[32,128,256]{2,1,0:T(8,128)} fusion(bf16[32,128,256]{2,1,0:T(8,128)(2,1)S(1)} %gather_fusion, pred[32]{0:T(512)(128)(4,1)S(1)} %get-tuple-element.169, pred[32]{0:T(512)(128)(4,1)S(1)} %get-tuple-element.170, bf16[96,128,128]{2,1,0:T(8,128)(2,1)} %get-tuple-element.198, s32[]{:T(128)S(6)} %select_n.82), kind=kOutput, calls=%fused_computation.2.clone.1 | convolution fusion | flops 270532608 | bytes 7340100 | tf_op jit(solution)/shard_map/while/body/kab,kbf->kaf/dot_general | solution.py:17
  58.9 9.5 %scatter_fusion = f32[32,128,256]{2,1,0:T(8,128)} fusion(f32[32,128,256]{2,1,0:T(8,128)} %get-tuple-element.183, s32[32]{0:T(128)S(1)} %compare_select_fusion.8, f32[32,128,256]{2,1,0:T(8,128)} %convolution_select_fusion.2), kind=kCustom, calls=%fused_computation.1.clone.1 | custom fusion | flops 1048576 | bytes 12583040 | tf_op jit(solution)/shard_map/while/body/scatter-add | solution.py:22
  68.4 0.0 reduce-scatter.2.cloned.1.call-update
  68.4 267.0 %reduce-scatter.2.cloned.1.call-done = f32[64,256]{1,0:T(8,128)} async-done(((f32[4096,256]{1,0:T(8,128)}), f32[64,256]{1,0:T(8,128)}) %reduce-scatter.2.cloned.1.call-update) | async-done | bytes 65552 | tf_op jit(solution)/shard_map/reduce_scatter | solution.py:42
  335.4 0.0 copy-done
  335.4 1.6 fusion.6
  (2 shorter events, 0.0 us)
Async XLA Ops:
  6.5 328.9 %copy-start = (bf16[256,256]{1,0:T(8,128)(2,1)S(1)}, bf16[256,256]{1,0:T(8,128)(2,1)}, u32[]{:S(2)}) copy-start(bf16[256,256]{1,0:T(8,128)(2,1)} %param.11) | copy-start | bytes 393220
  6.5 31.9 %copy-start.1 = (s32[1,1,96]{2,1,0:T(1,128)S(1)}, s32[1,1,96]{2,1,0:T(1,128)}, u32[]{:S(2)}) copy-start(s32[1,1,96]{2,1,0:T(1,128)} %param.9) | copy-start | bytes 1156
  6.5 328.9 %reduce-scatter.2.cloned.1.call-start = ((), (), s32[]{:S(2)}) async-start(), calls=%async_computation.1 | async-start | bytes 4259840 | tf_op jit(solution)/shard_map/reduce_scatter | solution.py:42
Sparse Core Ops, SparseCore 0:
  68.5 266.8 reduce-scatter.1
where the time goes:
time: 344 us
  waiting for transfers between devices  267 us (78%)
  blocking collectives  28.8 us (8%)
  other arithmetic  20.6 us (6%)
  between operations  14.1 us (4%)
  matrix products  9.49 us (3%)
  local copies, waits for them, and re-layouts  3.82 us (1%)
    reduce_scatter x1, waiting for transfers between devices, per_device(): summed = lax.psum_scatter(flat_rows, 'row', scatter_dimension=0, tiled=True)  267 us
    all_gather x1, blocking collectives, per_device(): gathered = lax.all_gather(features, 'col', axis=0, tiled=True)  28.8 us
    scatter-add x2, other arithmetic, add_block(): return running.at[row_ids].add(masked)  19 us
    dot_general x2, matrix products, add_block(): jnp.einsum('kab,kbf->kaf', tile_block, sources, preferred_element_type=jn...  7.88 us
  transfers between devices with their start and end apart: 1, of which 1 were waited for; matrix products, arithmetic and copies ran while one was open for 0% of the time, Pallas kernels for 0%

commit v1 on v0

v1 whole, which is shorter than its diff:
```python
import functools

import jax
import jax.numpy as jnp
from jax import lax
from jax.experimental import pallas as pl
from jax.experimental.pallas import tpu as pltpu
from jax.sharding import PartitionSpec as P

MESH = pl.DeviceIdType.MESH
RING = 8
TILE = 128
MAST = 64
HALF = MAST // 2
SUBS = 4
F32 = jnp.float32
BF16 = jnp.bfloat16


def place_of(offset):
    far = offset // 4
    return far * (2 * offset - 8) + (1 - far) * (7 - 2 * offset)


def kernel(
    features, tiles, places, counts, weight, out,
    x_all, held, spots, limit, w_vmem, dense, part,
    send_far, recv_far, send_ring, recv_ring, send_last, recv_last, own,
    load_sem, gather_send, gather_recv, twin_send, twin_recv,
    far_send, far_recv, ring_send, ring_recv, last_send, last_recv,
):
    row = lax.axis_index("row")
    col = lax.axis_index("col")
    mz, mx = row // RING, row % RING
    my, core = col // 2, col % 2
    slots = tiles.shape[2]

    def around(axis, step):
        if axis == 0:
            return (((mz + step + RING) % RING) * RING + mx, col)
        if axis == 1:
            return (mz * RING + (mx + step + RING) % RING, col)
        return (row, ((my + step + RING) % RING) * 2 + core)

    twin = (row, my * 2 + 1 - core)

    loads = [
        pltpu.make_async_copy(features, x_all.at[col], load_sem.at[0]),
        pltpu.make_async_copy(places.at[0], spots, load_sem.at[1]),
        pltpu.make_async_copy(counts, limit, load_sem.at[2]),
        pltpu.make_async_copy(tiles.at[0, 0], held.at[pl.ds(0, slots)], load_sem.at[3]),
        pltpu.make_async_copy(weight, w_vmem, load_sem.at[4]),
    ]
    for load in loads:
        load.start()

    barrier = pltpu.get_barrier_semaphore()
    for axis in range(3):
        for step in range(1, RING):
            pl.semaphore_signal(barrier, inc=1, device_id=around(axis, step), device_id_type=MESH)
    pl.semaphore_signal(barrier, inc=1, device_id=twin, device_id_type=MESH)

    def remote(src, dst, send, recv, to):
        return pltpu.make_async_remote_copy(
            src_ref=src, dst_ref=dst, send_sem=send, recv_sem=recv, device_id=to, device_id_type=MESH
        )

    def gather_copy(step):
        mine = x_all.at[col]
        return remote(mine, mine, gather_send.at[step], gather_recv.at[step], around(2, step))

    def twin_copy(step):
        block = x_all.at[((my - step + RING) % RING) * 2 + core]
        return remote(block, block, twin_send.at[step], twin_recv.at[step], twin)

    loads[0].wait()
    pl.semaphore_wait(barrier, 3 * (RING - 1) + 1)
    for step in (4, 3, 5, 2, 6, 1, 7):
        gather_copy(step).start()
    twin_copy(0).start()

    held[slots] = jnp.zeros((TILE, TILE), BF16)
    for load in loads[1:]:
        load.wait()
    own_count = limit[0, 0]

    def fill(i, pointer):
        tz = i // 4
        oz = (tz - mz + RING) % RING
        qz = place_of(oz)
        for j in range(8):
            at = jnp.minimum(pointer, slots - 1)
            hit = jnp.where((spots[0, at] == i * 8 + j) & (pointer < own_count), 1, 0)
            slot = slots + hit * (pointer - slots)
            pointer = pointer + hit
            for side in range(2):
                ox = (2 * (i % 4) + side - mx + RING) % RING
                qx = place_of(ox)
                first = side * MAST
                lanes = pl.ds(j * TILE, TILE)
                dense[0, oz, qx, :, lanes] = held[slot, pl.ds(first, HALF), :]
                dense[1, ox, qz, :, lanes] = held[slot, pl.ds(first + HALF, HALF), :]
        return pointer

    lax.fori_loop(0, 32, fill, jnp.int32(0))

    for step in (1, 7, 2, 6, 3, 5, 4):
        gather_copy(step).wait_recv()
        twin_copy(step).start()
    for step in (0, 1, 7, 2, 6, 3, 5, 4):
        twin_copy(step).wait_recv()

    def compute(axis, offset):
        lhs = dense[axis, offset].reshape(RING * HALF, -1)
        rhs = x_all[...].reshape(-1, x_all.shape[-1])
        value = jnp.dot(lhs, rhs, preferred_element_type=F32)
        part[axis, offset] = value.reshape(part.shape[2:])

    def far_copy(d, u):
        return remote(
            send_far.at[d, u], recv_far.at[d, u], far_send.at[d, u], far_recv.at[d, u],
            around(d // 2, 2 - 4 * (d % 2)),
        )

    def ring_copy(d, step, sub):
        return remote(
            send_ring.at[d, step, sub], recv_ring.at[d, step, sub],
            ring_send.at[d, step, sub], ring_recv.at[d, step, sub],
            around(d // 2, 1 - 2 * (d % 2)),
        )

    def last_copy(axis, offset):
        return remote(
            send_last.at[axis, offset], recv_last.at[axis, offset],
            last_send.at[axis, offset], last_recv.at[axis, offset], around(1 - axis, offset),
        )

    def toward(d, steps):
        return steps if d % 2 == 0 else RING - steps

    for axis in range(2):
        compute(axis, 4)
        for d in (2 * axis, 2 * axis + 1):
            for u in range(2):
                send_far[d, u] = part[axis, 4, u + 2 * (d % 2)].astype(BF16)
                far_copy(d, u).start()
    for d in range(4):
        offset = toward(d, 3)
        compute(d // 2, offset)
        for sub in range(SUBS):
            send_ring[d, 0, sub] = part[d // 2, offset, sub].astype(BF16)
            ring_copy(d, 0, sub).start()

    for step in (1, 2):
        for d in range(4):
            compute(d // 2, toward(d, 3 - step))
        for sub in range(SUBS):
            for d in range(4):
                value = part[d // 2, toward(d, 3 - step), sub]
                if step == 1 and sub // 2 == d % 2:
                    far_copy(d, sub % 2).wait_recv()
                    value = value + recv_far[d, sub % 2].astype(F32)
                ring_copy(d, step - 1, sub).wait_recv()
                value = value + recv_ring[d, step - 1, sub].astype(F32)
                send_ring[d, step, sub] = value.astype(BF16)
                ring_copy(d, step, sub).start()

    for axis in range(2):
        compute(axis, 0)
    for sub in range(SUBS):
        for axis in range(2):
            value = part[axis, 0, sub]
            for d in (2 * axis, 2 * axis + 1):
                ring_copy(d, 2, sub).wait_recv()
                value = value + recv_ring[d, 2, sub].astype(F32)
            send_last[axis, 4 + sub] = value[:HALF].astype(BF16)
            last_copy(axis, 4 + sub).start()
            if sub < SUBS - 1:
                send_last[axis, 3 - sub] = value[HALF:].astype(BF16)
                last_copy(axis, 3 - sub).start()
            else:
                own[axis] = value[HALF:]

    for axis in range(2):
        total = own[axis]
        for offset in (4, 3, 5, 2, 6, 1, 7):
            last_copy(axis, offset).wait_recv()
            total = total + recv_last[axis, offset].astype(F32)
        own[axis] = total
    aggregated = own[...].reshape(MAST, -1).astype(BF16)
    hidden = jnp.dot(aggregated, w_vmem[...], preferred_element_type=F32)
    out[...] = jnp.maximum(hidden, 0.0).astype(BF16)

    for step in range(1, RING):
        gather_copy(step).wait_send()
    for step in range(RING):
        twin_copy(step).wait_send()
    for d in range(4):
        for u in range(2):
            far_copy(d, u).wait_send()
        for step in range(3):
            for sub in range(SUBS):
                ring_copy(d, step, sub).wait_send()
    for axis in range(2):
        for offset in range(1, RING):
            last_copy(axis, offset).wait_send()


def per_device(features, tiles, places, counts, weight):
    width = features.shape[1]
    slots = tiles.shape[2]
    piece = (2 * HALF, width)
    dma = pltpu.SemaphoreType.DMA
    anywhere = pl.BlockSpec(memory_space=pltpu.HBM)
    return pl.pallas_call(
        kernel,
        out_shape=jax.ShapeDtypeStruct(features.shape, BF16),
        in_specs=[anywhere] * 5,
        out_specs=pl.BlockSpec(memory_space=pltpu.VMEM),
        scratch_shapes=[
            pltpu.VMEM((2 * RING, MAST, width), BF16),
            pltpu.VMEM((slots + 1, TILE, TILE), BF16),
            pltpu.SMEM((1, slots), jnp.int32),
            pltpu.SMEM((1, 1), jnp.int32),
            pltpu.VMEM(weight.shape, BF16),
            pltpu.VMEM((2, RING, RING, HALF, RING * TILE), BF16),
            pltpu.VMEM((2, RING, SUBS) + piece, F32),
            pltpu.VMEM((4, 2) + piece, BF16),
            pltpu.VMEM((4, 2) + piece, BF16),
            pltpu.VMEM((4, 3, SUBS) + piece, BF16),
            pltpu.VMEM((4, 3, SUBS) + piece, BF16),
            pltpu.VMEM((2, RING, HALF, width), BF16),
            pltpu.VMEM((2, RING, HALF, width), BF16),
            pltpu.VMEM((2, HALF, width), F32),
            dma((5,)),
            dma((RING,)),
            dma((RING,)),
            dma((RING,)),
            dma((RING,)),
            dma((4, 2)),
            dma((4, 2)),
            dma((4, 3, SUBS)),
            dma((4, 3, SUBS)),
            dma((2, RING)),
            dma((2, RING)),
        ],
        compiler_params=pltpu.CompilerParams(
            collective_id=0, has_side_effects=True, vmem_limit_bytes=60 * 2**20
        ),
    )(features, tiles, places, counts, weight)


def solution(mesh):
    return jax.shard_map(
        per_device,
        mesh=mesh,
        in_specs=(
            P(("row", "col"), None),
            P("row", "col", None, None, None),
            P("row", "col", None),
            P("row", "col"),
            P(),
        ),
        out_specs=P(("row", "col"), None),
        check_vma=False,
    )
```

time: 344 us -> 55.2 us (0.16)
  the two profiles are of different devices: /device:TPU:16 before, /device:TPU:1 now
where the time goes in v1:
time: 55.2 us; the launch traced here: 55 us
  Pallas kernels  52.9 us (96%)
  local copies, waits for them, and re-layouts  1.38 us (2%)
  between operations  0.66 us (1%)
    pallas_call x1, Pallas kernels, per_device(): pl.pallas_call(kernel, out_shape=jax.ShapeDtypeStruct(features.shape, BF1...  52.9 us
    unnamed x1, local copies, waits for them, and re-layouts  1.38 us

profile of v1, /device:TPU:1, one launch (start us, length us, event | category | flops | bytes accessed | tf_op | source)
XLA Modules:
  0.0 55.0 jit_solution(160703951837052160)
XLA Ops:
  0.7 52.9 %shard_map.55 = bf16[64,256]{1,0:T(8,128)(2,1)} custom-call(bf16[64,256]{1,0:T(8,128)(2,1)} %features.1, bf16[1,1,96,128,128]{4,3,2,1,0:T(8,128)(2,1)} %tiles.1, s32[1,1,96]{2,1,0:T(1,128)} %places.1, s32[1,1]{1,0:T(1,128)S(6)} %copy.7.counts, bf16[256,256]{1,0:T(8,128)(2,1)} %weight.1), custom_call_target="tpu_custom_call" | custom-call | tf_op jit(solution)/shard_map/pallas_call | solution.py:215
  53.6 1.4 %copy.8 = bf16[64,256]{1,0:T(8,128)(2,1)} copy(bf16[64,256]{1,0:T(8,128)(2,1)} %shard_map.55) | data formatting | bytes 65536

commit v2 on v1

v2 whole, which is shorter than its diff:
```python
import functools

import jax
import jax.numpy as jnp
from jax import lax
from jax.experimental import pallas as pl
from jax.experimental.pallas import tpu as pltpu
from jax.sharding import PartitionSpec as P

MESH = pl.DeviceIdType.MESH
RING = 8
TILE = 128
MAST = 64
HALF = MAST // 2
SIDES = 2
SUB = RING * HALF // 2
FAR_FIRST = (4, 3, 5, 2, 6, 1, 7)
NEAR_FIRST = (1, 7, 2, 6, 3, 5, 4)
ORDER = (4, 3, 5, 2, 6, 1, 7, 0)
F32 = jnp.float32
BF16 = jnp.bfloat16


def place_of(offset):
    far = offset // 4
    return far * (2 * offset - 8) + (1 - far) * (7 - 2 * offset)


def kernel(
    features, tiles, places, counts, weight, out,
    x_all, held, spots, limit, w_vmem, dense, part,
    send_far, recv_far, send_ring, recv_ring, send_last, recv_last, own,
    load_sem, gather_send, gather_recv, pair_send, pair_recv, twin_send, twin_recv,
    far_send, far_recv, ring_send, ring_recv, last_send, last_recv,
):
    row = lax.axis_index("row")
    col = lax.axis_index("col")
    mz, mx = row // RING, row % RING
    my, core = col // 2, col % 2
    slots = tiles.shape[2]
    lanes = features.shape[1] // SIDES

    def around(axis, step):
        if axis == 0:
            return (((mz + step + RING) % RING) * RING + mx, col)
        return (mz * RING + (mx + step + RING) % RING, col)

    def along(step, which):
        return (row, ((my + step + RING) % RING) * 2 + which)

    twin = (row, my * 2 + 1 - core)

    loads = [
        pltpu.make_async_copy(features.at[:, pl.ds(h * lanes, lanes)], x_all.at[h, col], load_sem.at[h])
        for h in range(SIDES)
    ]
    loads += [
        pltpu.make_async_copy(tiles.at[0, 0], held.at[pl.ds(0, slots)], load_sem.at[2]),
        pltpu.make_async_copy(places.at[0], spots, load_sem.at[3]),
        pltpu.make_async_copy(counts, limit, load_sem.at[4]),
        pltpu.make_async_copy(weight, w_vmem, load_sem.at[5]),
    ]
    for load in loads:
        load.start()

    barrier = pltpu.get_barrier_semaphore()

    def greet(to):
        pl.semaphore_signal(barrier, inc=1, device_id=to, device_id_type=MESH)

    @pl.when(core == 1)
    def _():
        for step in FAR_FIRST:
            greet(along(step, 0))
            greet(along(step, 1))

    for axis in range(2):
        for step in (2, 6, 1, 7):
            greet(around(axis, step))
    greet(twin)

    def remote(src, dst, send, recv, to):
        return pltpu.make_async_remote_copy(
            src_ref=src, dst_ref=dst, send_sem=send, recv_sem=recv, device_id=to, device_id_type=MESH
        )

    def gather_copy(h, step):
        mine = x_all.at[h, col]
        return remote(mine, mine, gather_send.at[h, step], gather_recv.at[h, core, step], along(step, 1))

    def arrival(h, which, step):
        block = x_all.at[h, ((my - step + RING) % RING) * 2 + which]
        return remote(block, block, gather_send.at[h, step], gather_recv.at[h, which, step], twin)

    def pair_copy(h, step):
        pair = x_all.at[h, pl.ds(((my - step + RING) % RING) * 2, 2)]
        return remote(pair, pair, pair_send.at[h, step], pair_recv.at[h, step], twin)

    def twin_copy(h):
        mine = x_all.at[h, col]
        return remote(mine, mine, twin_send.at[h], twin_recv.at[h], twin)

    for h in range(SIDES):
        loads[h].wait()
    pl.semaphore_wait(barrier, 16)
    for h in range(SIDES):
        for step in FAR_FIRST:
            gather_copy(h, step).start()
        twin_copy(h).start()

    held[slots] = jnp.zeros((TILE, TILE), BF16)
    for load in loads[SIDES:]:
        load.wait()
    own_count = limit[0, 0]

    def fill(i, pointer):
        oz = (i // 4 - mz + RING) % RING
        qz = place_of(oz)
        for j in range(8):
            at = jnp.minimum(pointer, slots - 1)
            hit = jnp.where((spots[0, at] == i * 8 + j) & (pointer < own_count), 1, 0)
            slot = slots + hit * (pointer - slots)
            pointer = pointer + hit
            for side in range(2):
                ox = (2 * (i % 4) + side - mx + RING) % RING
                qx = place_of(ox)
                first = side * MAST
                columns = pl.ds(j * TILE, TILE)
                dense[0, oz, qx, :, columns] = held[slot, pl.ds(first, HALF), :]
                dense[1, ox, qz, :, columns] = held[slot, pl.ds(first + HALF, HALF), :]
        return pointer

    lax.fori_loop(0, 32, fill, jnp.int32(0))

    def collect(h):
        @pl.when(core == 1)
        def _():
            for step in NEAR_FIRST:
                for which in range(2):
                    arrival(h, which, step).wait_recv()
                pair_copy(h, step).start()

        @pl.when(core == 0)
        def _():
            for step in NEAR_FIRST:
                pair_copy(h, step).wait_recv()

        twin_copy(h).wait_recv()

    def product(axis, offset, rhs):
        lhs = dense[axis, offset].reshape(RING * HALF, -1)
        return jnp.dot(lhs, rhs, preferred_element_type=F32)

    def source(h):
        return x_all[h].reshape(-1, lanes)

    def far_copy(d, h):
        return remote(
            send_far.at[d, h], recv_far.at[d, h], far_send.at[d, h], far_recv.at[d, h],
            around(d // 2, 2 - 4 * (d % 2)),
        )

    def ring_copy(d, step, h, sub):
        return remote(
            send_ring.at[d, step, h, sub], recv_ring.at[d, step, h, sub],
            ring_send.at[d, step, h, sub], ring_recv.at[d, step, h, sub],
            around(d // 2, 1 - 2 * (d % 2)),
        )

    def last_copy(axis, offset, h):
        return remote(
            send_last.at[axis, offset, h], recv_last.at[axis, offset, h],
            last_send.at[axis, offset, h], last_recv.at[axis, offset, h], around(1 - axis, offset),
        )

    def toward(d, steps):
        return steps if d % 2 == 0 else RING - steps

    for h in range(SIDES):
        collect(h)
        for axis in range(2):
            value = product(axis, 4, source(h)).astype(BF16).reshape(2, SUB, lanes)
            for d in (2 * axis, 2 * axis + 1):
                send_far[d, h] = value[d % 2]
                far_copy(d, h).start()
        for d in range(4):
            value = product(d // 2, toward(d, 3), source(h)).astype(BF16).reshape(2, SUB, lanes)
            for sub in range(2):
                send_ring[d, 0, h, sub] = value[sub]
                ring_copy(d, 0, h, sub).start()

    def compute(axis, offset):
        rhs = jnp.concatenate([source(h) for h in range(SIDES)], axis=1)
        value = product(axis, offset, rhs)
        for h in range(SIDES):
            part[axis, offset, h] = value[:, h * lanes : (h + 1) * lanes].reshape(2, SUB, lanes)

    for step in (1, 2):
        for d in range(4):
            compute(d // 2, toward(d, 3 - step))
        for h in range(SIDES):
            for sub in range(2):
                for d in range(4):
                    value = part[d // 2, toward(d, 3 - step), h, sub]
                    if step == 1 and sub == d % 2:
                        far_copy(d, h).wait_recv()
                        value = value + recv_far[d, h].astype(F32)
                    ring_copy(d, step - 1, h, sub).wait_recv()
                    value = value + recv_ring[d, step - 1, h, sub].astype(F32)
                    send_ring[d, step, h, sub] = value.astype(BF16)
                    ring_copy(d, step, h, sub).start()

    for axis in range(2):
        compute(axis, 0)
    for h in range(SIDES):
        for sub in range(2):
            for axis in range(2):
                value = part[axis, 0, h, sub]
                for d in (2 * axis, 2 * axis + 1):
                    ring_copy(d, 2, h, sub).wait_recv()
                    value = value + recv_ring[d, 2, h, sub].astype(F32)
                for t in range(4):
                    offset = ORDER[4 * sub + t]
                    piece = value[t * HALF : (t + 1) * HALF]
                    if offset:
                        send_last[axis, offset, h] = piece.astype(BF16)
                        last_copy(axis, offset, h).start()
                    else:
                        own[axis, h] = piece

    for h in range(SIDES):
        for axis in range(2):
            total = own[axis, h]
            for offset in FAR_FIRST:
                last_copy(axis, offset, h).wait_recv()
                total = total + recv_last[axis, offset, h].astype(F32)
            own[axis, h] = total
    aggregated = jnp.concatenate([own[:, h].reshape(MAST, lanes) for h in range(SIDES)], axis=1).astype(BF16)
    hidden = jnp.dot(aggregated, w_vmem[...], preferred_element_type=F32)
    out[...] = jnp.maximum(hidden, 0.0).astype(BF16)

    for h in range(SIDES):
        twin_copy(h).wait_send()
        for step in range(1, RING):
            gather_copy(h, step).wait_send()
        for d in range(4):
            far_copy(d, h).wait_send()
            for step in range(3):
                for sub in range(2):
                    ring_copy(d, step, h, sub).wait_send()
        for axis in range(2):
            for offset in range(1, RING):
                last_copy(axis, offset, h).wait_send()

    @pl.when(core == 1)
    def _():
        for h in range(SIDES):
            for step in range(1, RING):
                pair_copy(h, step).wait_send()


def per_device(features, tiles, places, counts, weight):
    width = features.shape[1]
    slots = tiles.shape[2]
    lanes = width // SIDES
    piece = (SUB, lanes)
    dma = pltpu.SemaphoreType.DMA
    anywhere = pl.BlockSpec(memory_space=pltpu.HBM)
    return pl.pallas_call(
        kernel,
        out_shape=jax.ShapeDtypeStruct(features.shape, BF16),
        in_specs=[anywhere] * 5,
        out_specs=pl.BlockSpec(memory_space=pltpu.VMEM),
        scratch_shapes=[
            pltpu.VMEM((SIDES, 2 * RING, MAST, lanes), BF16),
            pltpu.VMEM((slots + 1, TILE, TILE), BF16),
            pltpu.SMEM((1, slots), jnp.int32),
            pltpu.SMEM((1, 1), jnp.int32),
            pltpu.VMEM(weight.shape, BF16),
            pltpu.VMEM((2, RING, RING, HALF, RING * TILE), BF16),
            pltpu.VMEM((2, RING, SIDES, 2) + piece, F32),
            pltpu.VMEM((4, SIDES) + piece, BF16),
            pltpu.VMEM((4, SIDES) + piece, BF16),
            pltpu.VMEM((4, 3, SIDES, 2) + piece, BF16),
            pltpu.VMEM((4, 3, SIDES, 2) + piece, BF16),
            pltpu.VMEM((2, RING, SIDES, HALF, lanes), BF16),
            pltpu.VMEM((2, RING, SIDES, HALF, lanes), BF16),
            pltpu.VMEM((2, SIDES, HALF, lanes), F32),
            dma((6,)),
            dma((SIDES, RING)),
            dma((SIDES, 2, RING)),
            dma((SIDES, RING)),
            dma((SIDES, RING)),
            dma((SIDES,)),
            dma((SIDES,)),
            dma((4, SIDES)),
            dma((4, SIDES)),
            dma((4, 3, SIDES, 2)),
            dma((4, 3, SIDES, 2)),
            dma((2, RING, SIDES)),
            dma((2, RING, SIDES)),
        ],
        compiler_params=pltpu.CompilerParams(
            collective_id=0, has_side_effects=True, vmem_limit_bytes=60 * 2**20
        ),
    )(features, tiles, places, counts, weight)


def solution(mesh):
    return jax.shard_map(
        per_device,
        mesh=mesh,
        in_specs=(
            P(("row", "col"), None),
            P("row", "col", None, None, None),
            P("row", "col", None),
            P("row", "col"),
            P(),
        ),
        out_specs=P(("row", "col"), None),
        check_vma=False,
    )
```

time: 55.2 us -> 52.9 us (0.958)
  the two profiles are of different devices: /device:TPU:1 before, /device:TPU:4 now
where the time goes in v2:
time: 52.9 us; the launch traced here: 52.5 us
  Pallas kernels  50.4 us (95%)
  local copies, waits for them, and re-layouts  1.38 us (3%)
  between operations  0.66 us (1%)
    pallas_call x1, Pallas kernels, per_device(): pl.pallas_call(kernel, out_shape=jax.ShapeDtypeStruct(features.shape, BF1...  50.4 us
    unnamed x1, local copies, waits for them, and re-layouts  1.38 us

profile of v2, /device:TPU:4, one launch (start us, length us, event | category | flops | bytes accessed | tf_op | source)
XLA Modules:
  0.0 52.5 jit_solution(17151498110439382044)
XLA Ops:
  0.7 50.4 %shard_map.55 = bf16[64,256]{1,0:T(8,128)(2,1)} custom-call(bf16[64,256]{1,0:T(8,128)(2,1)} %features.1, bf16[1,1,96,128,128]{4,3,2,1,0:T(8,128)(2,1)} %tiles.1, s32[1,1,96]{2,1,0:T(1,128)} %places.1, s32[1,1]{1,0:T(1,128)S(6)} %copy.7.counts, bf16[256,256]{1,0:T(8,128)(2,1)} %weight.1), custom_call_target="tpu_custom_call" | custom-call | tf_op jit(solution)/shard_map/pallas_call | solution.py:269
  51.1 1.4 %copy.8 = bf16[64,256]{1,0:T(8,128)(2,1)} copy(bf16[64,256]{1,0:T(8,128)(2,1)} %shard_map.55) | data formatting | bytes 65536

commit v3 on v2

v3 whole, which is shorter than its diff:
```python
import functools

import jax
import jax.numpy as jnp
from jax import lax
from jax.experimental import pallas as pl
from jax.experimental.pallas import tpu as pltpu
from jax.sharding import PartitionSpec as P

MESH = pl.DeviceIdType.MESH
RING = 8
TILE = 128
MAST = 64
HALF = MAST // 2
SIDES = 2
SUBS = 2
SUB = RING * HALF // SUBS
FAR_FIRST = (4, 3, 5, 2, 6, 1, 7)
NEAR_FIRST = (1, 7, 2, 6, 3, 5, 4)
ORDER = (4, 3, 5, 2, 6, 1, 7, 0)
F32 = jnp.float32
BF16 = jnp.bfloat16


def place_of(offset):
    far = offset // 4
    return far * (2 * offset - 8) + (1 - far) * (7 - 2 * offset)


def kernel(
    features, tiles, places, counts, weight, out,
    x_all, held, spots, limit, w_vmem, dense, part,
    send_far, recv_far, send_ring, recv_ring, send_last, recv_last, own,
    load_sem, gather_send, gather_recv, pair_send, pair_recv, twin_send, twin_recv,
    far_send, far_recv, ring_send, ring_recv, last_send, last_recv,
):
    row = lax.axis_index("row")
    col = lax.axis_index("col")
    mz, mx = row // RING, row % RING
    my, core = col // 2, col % 2
    slots = tiles.shape[2]
    lanes = features.shape[1] // SIDES

    def around(axis, step):
        if axis == 0:
            return (((mz + step + RING) % RING) * RING + mx, col)
        return (mz * RING + (mx + step + RING) % RING, col)

    def along(step, which):
        return (row, ((my + step + RING) % RING) * 2 + which)

    twin = (row, my * 2 + 1 - core)

    def half(h):
        return features.at[:, pl.ds(h * lanes, lanes)]

    loads = [pltpu.make_async_copy(half(h), x_all.at[h, col], load_sem.at[h]) for h in range(SIDES)]
    loads += [
        pltpu.make_async_copy(tiles.at[0, 0], held.at[pl.ds(0, slots)], load_sem.at[2]),
        pltpu.make_async_copy(places.at[0], spots, load_sem.at[3]),
        pltpu.make_async_copy(counts, limit, load_sem.at[4]),
        pltpu.make_async_copy(weight, w_vmem, load_sem.at[5]),
    ]
    barrier = pltpu.get_barrier_semaphore()

    def greet(to):
        pl.semaphore_signal(barrier, inc=1, device_id=to, device_id_type=MESH)

    @pl.when(core == 1)
    def _():
        for step in FAR_FIRST:
            greet(along(step, 0))
            greet(along(step, 1))

    for axis in range(2):
        for step in (2, 6, 1, 7):
            greet(around(axis, step))
    greet(twin)

    def remote(src, dst, send, recv, to):
        return pltpu.make_async_remote_copy(
            src_ref=src, dst_ref=dst, send_sem=send, recv_sem=recv, device_id=to, device_id_type=MESH
        )

    def gather_copy(h, step):
        return remote(
            x_all.at[h, col], x_all.at[h, col], gather_send.at[0], gather_recv.at[h, step], along(step, 1)
        )

    def pair_of(h, step):
        return x_all.at[h, pl.ds(((my - step + RING) % RING) * 2, 2)]

    def arrival(h, step):
        return remote(pair_of(h, step), pair_of(h, step), gather_send.at[0], gather_recv.at[h, step], twin)

    def pair_copy(h, step):
        return remote(pair_of(h, step), pair_of(h, step), pair_send.at[0], pair_recv.at[h], twin)

    def all_of(ref, send, recv):
        return remote(ref, ref, send, recv, twin)

    def twin_copy(h):
        return remote(x_all.at[h, col], x_all.at[h, col], twin_send.at[h], twin_recv.at[h], twin)

    for load in loads:
        load.start()
    for h in range(SIDES):
        loads[h].wait()
    pl.semaphore_wait(barrier, 16)
    for h in range(SIDES):
        for step in FAR_FIRST:
            gather_copy(h, step).start()
        twin_copy(h).start()

    held[slots] = jnp.zeros((TILE, TILE), BF16)
    for load in loads[SIDES:]:
        load.wait()
    own_count = limit[0, 0]

    def fill(i, pointer):
        oz = (i // 4 - mz + RING) % RING
        qz = place_of(oz)
        for j in range(8):
            at = jnp.minimum(pointer, slots - 1)
            hit = jnp.where((spots[0, at] == i * 8 + j) & (pointer < own_count), 1, 0)
            slot = slots + hit * (pointer - slots)
            pointer = pointer + hit
            for side in range(2):
                ox = (2 * (i % 4) + side - mx + RING) % RING
                qx = place_of(ox)
                first = side * MAST
                columns = pl.ds(j * TILE, TILE)
                dense[0, oz, qx, :, columns] = held[slot, pl.ds(first, HALF), :]
                dense[1, ox, qz, :, columns] = held[slot, pl.ds(first + HALF, HALF), :]
        return pointer

    lax.fori_loop(0, 32, fill, jnp.int32(0))

    def collect(h):
        @pl.when(core == 1)
        def _():
            for step in NEAR_FIRST:
                arrival(h, step).wait_recv()
                pair_copy(h, step).start()

        @pl.when(core == 0)
        def _():
            pairs = x_all.at[h, pl.ds(0, 2 * (RING - 1))]
            all_of(pairs, pair_send.at[0], pair_recv.at[h]).wait_recv()

        twin_copy(h).wait_recv()

    def product(axis, offset, rhs):
        lhs = dense[axis, offset].reshape(RING * HALF, -1)
        return jnp.dot(lhs, rhs, preferred_element_type=F32)

    def source(h):
        return x_all[h].reshape(-1, lanes)

    def far_copy(d, h, u):
        return remote(
            send_far.at[d, h, u], recv_far.at[d, h, u], far_send.at[0], far_recv.at[d, h, u],
            around(d // 2, 2 - 4 * (d % 2)),
        )

    def ring_copy(d, slot, h, sub):
        return remote(
            send_ring.at[d, slot, h, sub], recv_ring.at[d, slot, h, sub],
            ring_send.at[0], ring_recv.at[d, slot, h, sub],
            around(d // 2, 1 - 2 * (d % 2)),
        )

    def last_copy(axis, offset, h):
        return remote(
            send_last.at[h, axis, offset], recv_last.at[h, axis, offset],
            last_send.at[0], last_recv.at[h], around(1 - axis, offset),
        )

    def toward(d, steps):
        return steps if d % 2 == 0 else RING - steps

    def products(h, offsets):
        values = [product(axis, offset, source(h)) for axis, offset in offsets]
        return [value.reshape(SUBS, SUB, lanes) for value in values]

    def keep(offsets):
        rhs = jnp.concatenate([source(h) for h in range(SIDES)], axis=1)
        for axis, offset in offsets:
            value = product(axis, offset, rhs)
            for h in range(SIDES):
                part[axis, offset, h] = value[:, h * lanes : (h + 1) * lanes].reshape(SUBS, SUB, lanes)

    def at_distance(steps):
        return [(d // 2, toward(d, steps)) for d in range(4)]

    def send_farthest(h):
        values = products(h, [(0, 4), (1, 4)])
        for d in range(4):
            for u in range(SUBS // 2):
                send_far[d, h, u] = values[d // 2][SUBS // 2 * (d % 2) + u].astype(BF16)
        for u in range(SUBS // 2):
            for d in range(4):
                far_copy(d, h, u).start()

    def send_fresh(h, steps, slot):
        values = products(h, at_distance(steps))
        for d in range(4):
            send_ring[d, slot, h] = values[d].astype(BF16)
        for sub in range(SUBS):
            for d in range(4):
                ring_copy(d, slot, h, sub).start()

    def pass_on(h, steps, slot):
        for sub in range(SUBS):
            for d in range(4):
                value = part[d // 2, toward(d, steps), h, sub]
                u = sub - SUBS // 2 * (d % 2)
                if slot == 0 and 0 <= u < SUBS // 2:
                    far_copy(d, h, u).wait_recv()
                    value = value + recv_far[d, h, u].astype(F32)
                ring_copy(d, slot, h, sub).wait_recv()
                value = value + recv_ring[d, slot, h, sub].astype(F32)
                send_ring[d, slot + 1, h, sub] = value.astype(BF16)
                ring_copy(d, slot + 1, h, sub).start()

    for h in range(SIDES):
        collect(h)
        send_farthest(h)
        send_fresh(h, 3, 0)
    keep(at_distance(2))
    pass_on(0, 2, 0)
    keep(at_distance(1))
    keep([(0, 0), (1, 0)])
    pass_on(1, 2, 0)
    for h in range(SIDES):
        pass_on(h, 1, 1)

    for h in range(SIDES):
        for sub in range(SUBS):
            for axis in range(2):
                value = part[axis, 0, h, sub]
                for d in (2 * axis, 2 * axis + 1):
                    ring_copy(d, 2, h, sub).wait_recv()
                    value = value + recv_ring[d, 2, h, sub].astype(F32)
                for t in range(SUB // HALF):
                    offset = ORDER[SUB // HALF * sub + t]
                    piece = value[t * HALF : (t + 1) * HALF]
                    if offset:
                        send_last[h, axis, offset] = piece.astype(BF16)
                        last_copy(axis, offset, h).start()
                    else:
                        own[axis, h] = piece

    for h in range(SIDES):
        all_of(recv_last.at[h, :, pl.ds(1, RING - 1)], last_send.at[0], last_recv.at[h]).wait_recv()
        for axis in range(2):
            total = own[axis, h]
            for offset in FAR_FIRST:
                total = total + recv_last[h, axis, offset].astype(F32)
            own[axis, h] = total
    aggregated = jnp.concatenate([own[:, h].reshape(MAST, lanes) for h in range(SIDES)], axis=1).astype(BF16)
    hidden = jnp.dot(aggregated, w_vmem[...], preferred_element_type=F32)
    out[...] = jnp.maximum(hidden, 0.0).astype(BF16)

    for h in range(SIDES):
        twin_copy(h).wait_send()
    all_of(x_all.at[:, pl.ds(0, RING - 1)], gather_send.at[0], gather_recv.at[0, 0]).wait_send()
    all_of(send_last.at[:, :, pl.ds(1, RING - 1)], last_send.at[0], last_recv.at[0]).wait_send()
    all_of(send_far, far_send.at[0], far_recv.at[0, 0, 0]).wait_send()
    all_of(send_ring, ring_send.at[0], ring_recv.at[0, 0, 0, 0]).wait_send()

    @pl.when(core == 1)
    def _():
        pairs = x_all.at[:, pl.ds(0, 2 * (RING - 1))]
        all_of(pairs, pair_send.at[0], pair_recv.at[0]).wait_send()


def per_device(features, tiles, places, counts, weight):
    width = features.shape[1]
    slots = tiles.shape[2]
    lanes = width // SIDES
    piece = (SUB, lanes)
    dma = pltpu.SemaphoreType.DMA
    anywhere = pl.BlockSpec(memory_space=pltpu.HBM)
    return pl.pallas_call(
        kernel,
        out_shape=jax.ShapeDtypeStruct(features.shape, BF16),
        in_specs=[anywhere] * 5,
        out_specs=pl.BlockSpec(memory_space=pltpu.VMEM),
        scratch_shapes=[
            pltpu.VMEM((SIDES, 2 * RING, MAST, lanes), BF16),
            pltpu.VMEM((slots + 1, TILE, TILE), BF16),
            pltpu.SMEM((1, slots), jnp.int32),
            pltpu.SMEM((1, 1), jnp.int32),
            pltpu.VMEM(weight.shape, BF16),
            pltpu.VMEM((2, RING, RING, HALF, RING * TILE), BF16),
            pltpu.VMEM((2, RING, SIDES, SUBS) + piece, F32),
            pltpu.VMEM((4, SIDES, SUBS // 2) + piece, BF16),
            pltpu.VMEM((4, SIDES, SUBS // 2) + piece, BF16),
            pltpu.VMEM((4, 3, SIDES, SUBS) + piece, BF16),
            pltpu.VMEM((4, 3, SIDES, SUBS) + piece, BF16),
            pltpu.VMEM((SIDES, 2, RING, HALF, lanes), BF16),
            pltpu.VMEM((SIDES, 2, RING, HALF, lanes), BF16),
            pltpu.VMEM((2, SIDES, HALF, lanes), F32),
            dma((6,)),
            dma((1,)),
            dma((SIDES, RING)),
            dma((1,)),
            dma((SIDES,)),
            dma((SIDES,)),
            dma((SIDES,)),
            dma((1,)),
            dma((4, SIDES, SUBS // 2)),
            dma((1,)),
            dma((4, 3, SIDES, SUBS)),
            dma((1,)),
            dma((SIDES,)),
        ],
        compiler_params=pltpu.CompilerParams(
            collective_id=0, has_side_effects=True, vmem_limit_bytes=55168 * 2**10
        ),
    )(features, tiles, places, counts, weight)


def solution(mesh):
    return jax.shard_map(
        per_device,
        mesh=mesh,
        in_specs=(
            P(("row", "col"), None),
            P("row", "col", None, None, None),
            P("row", "col", None),
            P("row", "col"),
            P(),
        ),
        out_specs=P(("row", "col"), None),
        check_vma=False,
    )
```

time: 52.9 us -> 50.2 us (0.949)
  Pallas kernels: 50.4 us -> 48.1 us
    pallas_call x1, Pallas kernels: 50.4 us -> 48.1 us  [per_device(): pl.pallas_call(kernel, out_shape=jax.ShapeDtypeStruct(features.shape, BF1...]
    unnamed x1 -> x3, local copies, waits for them, and re-layouts: 1.38 us -> 1.27 us
where the time goes in v3:
time: 50.2 us; the launch traced here: 50 us
  Pallas kernels  48.1 us (96%)
  local copies, waits for them, and re-layouts  1.27 us (3%)
  between operations  0.67 us (1%)
    pallas_call x1, Pallas kernels, per_device(): pl.pallas_call(kernel, out_shape=jax.ShapeDtypeStruct(features.shape, BF1...  48.1 us
    unnamed x3, local copies, waits for them, and re-layouts  1.27 us

profile of v3, /device:TPU:4, one launch (start us, length us, event | category | flops | bytes accessed | tf_op | source)
XLA Modules:
  0.0 50.0 jit_solution(6451578781319219282)
XLA Ops:
  0.7 0.0 copy-start
  0.7 0.6 %copy-done = s32[1,1,96]{2,1,0:T(1,128)S(1)} copy-done((s32[1,1,96]{2,1,0:T(1,128)S(1)}, s32[1,1,96]{2,1,0:T(1,128)}, u32[]{:S(2)}) %copy-start) | copy-done | bytes 408
  1.3 48.1 %shard_map.55 = bf16[64,256]{1,0:T(8,128)(2,1)S(1)} custom-call(bf16[64,256]{1,0:T(8,128)(2,1)} %features.1, bf16[1,1,96,128,128]{4,3,2,1,0:T(8,128)(2,1)} %tiles.1, s32[1,1,96]{2,1,0:T(1,128)S(1)} %copy-done, s32[1,1]{1,0:T(1,128)S(6)} %copy.7.counts, bf16[256,256]{1,0:T(8,128)(2,1)} %weight.1), custom_call_target="tpu_custom_call" | custom-call | tf_op jit(solution)/shard_map/pallas_call | solution.py:285
  49.4 0.6 %copy.8 = bf16[64,256]{1,0:T(8,128)(2,1)} copy(bf16[64,256]{1,0:T(8,128)(2,1)S(1)} %shard_map.55) | data formatting | bytes 65536
Async XLA Ops:
  0.7 0.7 %copy-start = (s32[1,1,96]{2,1,0:T(1,128)S(1)}, s32[1,1,96]{2,1,0:T(1,128)}, u32[]{:S(2)}) copy-start(s32[1,1,96]{2,1,0:T(1,128)} %places.1) | copy-start | bytes 1156

commit v4 on v3

--- a/solution.py
+++ b/solution.py
@@ -32,7 +32,7 @@
     x_all, held, spots, limit, w_vmem, dense, part,
     send_far, recv_far, send_ring, recv_ring, send_last, recv_last, own,
     load_sem, gather_send, gather_recv, pair_send, pair_recv, twin_send, twin_recv,
-    far_send, far_recv, ring_send, ring_recv, last_send, last_recv,
+    far_send, ring_send, ring_recv, last_send, last_recv,
 ):
     row = lax.axis_index("row")
     col = lax.axis_index("col")
@@ -159,16 +159,19 @@
 
     def far_copy(d, h, u):
         return remote(
-            send_far.at[d, h, u], recv_far.at[d, h, u], far_send.at[0], far_recv.at[d, h, u],
+            send_far.at[d, h, u], recv_far.at[d, h, u], far_send.at[0], ring_recv.at[d, 0, h, SUBS // 2 * (d % 2) + u],
             around(d // 2, 2 - 4 * (d % 2)),
         )
 
     def ring_copy(d, slot, h, sub):
         return remote(
             send_ring.at[d, slot, h, sub], recv_ring.at[d, slot, h, sub],
-            ring_send.at[0], ring_recv.at[d, slot, h, sub],
+            ring_send.at[0], ring_recv.at[d if slot < 2 else d - d % 2, slot, h, sub],
             around(d // 2, 1 - 2 * (d % 2)),
         )
+
+    def two_pieces(d, slot, h, sub):
+        return all_of(recv_ring.at[d, slot, h, pl.ds(0, 2)], ring_send.at[0], ring_recv.at[d, slot, h, sub])
 
     def last_copy(axis, offset, h):
         return remote(
@@ -216,9 +219,10 @@
                 value = part[d // 2, toward(d, steps), h, sub]
                 u = sub - SUBS // 2 * (d % 2)
                 if slot == 0 and 0 <= u < SUBS // 2:
-                    far_copy(d, h, u).wait_recv()
+                    two_pieces(d, 0, h, sub).wait_recv()
                     value = value + recv_far[d, h, u].astype(F32)
-                ring_copy(d, slot, h, sub).wait_recv()
+                else:
+                    ring_copy(d, slot, h, sub).wait_recv()
                 value = value + recv_ring[d, slot, h, sub].astype(F32)
                 send_ring[d, slot + 1, h, sub] = value.astype(BF16)
                 ring_copy(d, slot + 1, h, sub).start()
@@ -239,8 +243,8 @@
         for sub in range(SUBS):
             for axis in range(2):
                 value = part[axis, 0, h, sub]
+                two_pieces(2 * axis, 2, h, sub).wait_recv()
                 for d in (2 * axis, 2 * axis + 1):
-                    ring_copy(d, 2, h, sub).wait_recv()
                     value = value + recv_ring[d, 2, h, sub].astype(F32)
                 for t in range(SUB // HALF):
                     offset = ORDER[SUB // HALF * sub + t]
@@ -266,7 +270,7 @@
         twin_copy(h).wait_send()
     all_of(x_all.at[:, pl.ds(0, RING - 1)], gather_send.at[0], gather_recv.at[0, 0]).wait_send()
     all_of(send_last.at[:, :, pl.ds(1, RING - 1)], last_send.at[0], last_recv.at[0]).wait_send()
-    all_of(send_far, far_send.at[0], far_recv.at[0, 0, 0]).wait_send()
+    all_of(send_far, far_send.at[0], ring_recv.at[0, 0, 0, 0]).wait_send()
     all_of(send_ring, ring_send.at[0], ring_recv.at[0, 0, 0, 0]).wait_send()
 
     @pl.when(core == 1)
@@ -310,7 +314,6 @@
             dma((SIDES,)),
             dma((SIDES,)),
             dma((1,)),
-            dma((4, SIDES, SUBS // 2)),
             dma((1,)),
             dma((4, 3, SIDES, SUBS)),
             dma((1,)),

time: 50.2 us -> 50.1 us (level)
  no operation moved by 1% of the time
where the time goes in v4:
time: 50.1 us; the launch traced here: 50 us
  Pallas kernels  48 us (96%)
  local copies, waits for them, and re-layouts  1.27 us (3%)
  between operations  0.67 us (1%)
    pallas_call x1, Pallas kernels, per_device(): pl.pallas_call(kernel, out_shape=jax.ShapeDtypeStruct(features.shape, BF1...  48 us
    unnamed x3, local copies, waits for them, and re-layouts  1.27 us

profile of v4, /device:TPU:4, one launch (start us, length us, event | category | flops | bytes accessed | tf_op | source)
XLA Modules:
  0.0 50.0 jit_solution(9937753023628943504)
XLA Ops:
  0.7 0.0 copy-start
  0.7 0.6 %copy-done = s32[1,1,96]{2,1,0:T(1,128)S(1)} copy-done((s32[1,1,96]{2,1,0:T(1,128)S(1)}, s32[1,1,96]{2,1,0:T(1,128)}, u32[]{:S(2)}) %copy-start) | copy-done | bytes 408
  1.3 48.0 %shard_map.55 = bf16[64,256]{1,0:T(8,128)(2,1)S(1)} custom-call(bf16[64,256]{1,0:T(8,128)(2,1)} %features.1, bf16[1,1,96,128,128]{4,3,2,1,0:T(8,128)(2,1)} %tiles.1, s32[1,1,96]{2,1,0:T(1,128)S(1)} %copy-done, s32[1,1]{1,0:T(1,128)S(6)} %copy.7.counts, bf16[256,256]{1,0:T(8,128)(2,1)} %weight.1), custom_call_target="tpu_custom_call" | custom-call | tf_op jit(solution)/shard_map/pallas_call | solution.py:289
  49.3 0.6 %copy.8 = bf16[64,256]{1,0:T(8,128)(2,1)} copy(bf16[64,256]{1,0:T(8,128)(2,1)S(1)} %shard_map.55) | data formatting | bytes 65536
Async XLA Ops:
  0.7 0.7 %copy-start = (s32[1,1,96]{2,1,0:T(1,128)S(1)}, s32[1,1,96]{2,1,0:T(1,128)}, u32[]{:S(2)}) copy-start(s32[1,1,96]{2,1,0:T(1,128)} %places.1) | copy-start | bytes 1156
